TPU v7x, 32 devices: a whole 2x2x4 slice. The times are simulated.
32 devices in a mesh: groups: 2 (over x), blk: 16 (over z, y, core).
Axes of the slice: x: 2, y: 2, z: 4, core: 2. Of those that a mesh axis runs over, the one named last changes fastest.
Arguments:
- tokens: bfloat16 [3072, 16384], P('groups', 'blk'), parts along dimension 0, may hold values from -640 to 640, as said below
- norm_gain: bfloat16 [16384], P('blk'), may hold values from 0.099609375 to 1.8984375
- left_factor: bfloat16 [128, 128, 128], P('blk'), may hold values from -0.5 to 0.5
- right_factor: bfloat16 [128, 128, 128], P('blk'), may hold values from -0.5 to 0.5
- cotangent: bfloat16 [3072, 16384], P('groups', 'blk'), parts along dimension 0, may hold values from -6 to 6
Outputs:
- mixer_out: bfloat16 [3072, 16384], P('groups', 'blk'), parts along dimension 0
- grad_tokens: bfloat16 [3072, 16384], P('groups', 'blk'), parts along dimension 0
- grad_left: float32 [256, 128, 128], P(('groups', 'blk')), parts along dimension 0
- grad_right: float32 [256, 128, 128], P(('groups', 'blk')), parts along dimension 0
- grad_gain: float32 [32768], P(('groups', 'blk')), parts along dimension 0
There are 2 independent parts, one for each index of `groups`. A program takes and returns all parts, laid end to end along the dimension named above; an argument that names none is the same for every part. Nothing has to cross between parts.
Inputs may be any that keep to these rules, and one draw needn't show every extreme that they name: `tokens`: Real-valued activations.
All inputs are finite; a program needn't handle non-finite values.
Results may differ from a plain program's by a relative error of at most 0.0067.
Values may be sent and summed in bfloat16 or wider, within the bound.
A program may use at most 64 MiB of HBM per device.

v0:
```python
import jax
import jax.numpy as jnp
from jax import lax
from jax.sharding import PartitionSpec as P

D = 16384


epsilon = 1e-06


def gelu_slope(inputs_f):
    return (
        0.5 * (1.0 + lax.erf(inputs_f * 0.7071067811865476))
        + inputs_f * jnp.exp(-0.5 * inputs_f * inputs_f) * 0.3989422804014327
    )


def on_device(tokens, norm_gain, left_factor, right_factor, cotangent):
    row_count = tokens.shape[0]
    local_blocks = left_factor.shape[0]
    block_order = left_factor.shape[1]
    widened = tokens.astype(jnp.float32)
    square_sum = lax.psum(jnp.sum(widened * widened, axis=1), "blk")
    inverse_rms = lax.rsqrt(square_sum / D + epsilon)
    gain_wide = norm_gain.astype(jnp.float32)
    normed = (widened * inverse_rms[:, None] * gain_wide[None, :]).astype(jnp.bfloat16)
    blocks = normed.reshape(row_count, local_blocks, block_order)
    pre_act = jnp.einsum(
        "tbi,bij->btj", blocks, left_factor, preferred_element_type=jnp.float32
    ).astype(jnp.bfloat16)
    pre_piece = lax.all_to_all(pre_act, "blk", split_axis=2, concat_axis=0, tiled=True)
    active = jax.nn.gelu(pre_piece.astype(jnp.float32), approximate=False).astype(jnp.bfloat16)
    mixed_out = jnp.einsum(
        "btj,jbc->jtc", active, right_factor, preferred_element_type=jnp.float32
    ).astype(jnp.bfloat16)
    mixed_out = lax.all_to_all(mixed_out, "blk", split_axis=2, concat_axis=0, tiled=True)
    incoming = jnp.transpose(cotangent.reshape(row_count, -1, block_order), (1, 0, 2))
    grad_mixed = lax.all_to_all(incoming, "blk", split_axis=2, concat_axis=0, tiled=True)
    mixer_out = jnp.transpose(mixed_out, (1, 2, 0)).reshape(row_count, -1)
    grad_right = jnp.einsum("btj,ctj->jbc", active, grad_mixed, preferred_element_type=jnp.float32)
    grad_act = jnp.einsum(
        "ctj,jbc->btj", grad_mixed, right_factor, preferred_element_type=jnp.float32
    )
    grad_pre = (grad_act * gelu_slope(pre_piece.astype(jnp.float32))).astype(jnp.bfloat16)
    grad_back = lax.all_to_all(grad_pre, "blk", split_axis=0, concat_axis=2, tiled=True)
    grad_left = jnp.einsum("tbi,btj->bij", blocks, grad_back, preferred_element_type=jnp.float32)
    grad_normed = jnp.einsum(
        "btj,bij->tbi", grad_back, left_factor, preferred_element_type=jnp.float32
    ).reshape(row_count, -1)
    grad_gain = jnp.sum(grad_normed * widened * inverse_rms[:, None], axis=0)
    scaled = grad_normed * gain_wide[None, :]
    correction = lax.psum(jnp.sum(scaled * widened, axis=1), "blk")
    grad_tokens = (
        inverse_rms[:, None] * scaled - widened * (inverse_rms**3 * correction / D)[:, None]
    ).astype(jnp.bfloat16)
    return (mixer_out, grad_tokens, grad_left, grad_right, grad_gain)


def solution(mesh):
    placed = (
        P("groups", "blk"),
        P("blk"),
        P("blk", None, None),
        P("blk", None, None),
        P("groups", "blk"),
    )
    return jax.shard_map(
        on_device,
        mesh=mesh,
        in_specs=placed,
        out_specs=(
            P("groups", "blk"),
            P("groups", "blk"),
            P(("groups", "blk"), None, None),
            P(("groups", "blk"), None, None),
            P(("groups", "blk")),
        ),
        check_vma=False,
    )
```

profile of v0, /device:TPU:0, one launch (start us, length us, event | category | flops | bytes accessed | tf_op | source)
XLA Modules:
  0.0 426.4 jit_solution(11661673249517536958)
XLA Ops:
  0.6 0.0 copy-start
  0.6 0.7 convert_element_type.38
  1.4 2.6 fusion.9
  3.9 35.4 %psum.14 = f32[1536]{0:T(1024)S(1)} all-reduce(f32[1536]{0:T(1024)S(1)} %fusion.9), channel_id=1, replica_groups=mesh['groups'=2,'blk'=16] {'blk'}, use_global_device_ids=true, to_apply=%region_1.0 | all-reduce | flops 1536 | bytes 12288 | tf_op jit(solution)/shard_map/psum | solution.py:24
  39.4 4.3 %fusion.11 = bf16[1536,1024]{1,0:T(8,128)(2,1)} fusion(bf16[1536,1024]{1,0:T(8,128)(2,1)} %param.5, f32[1024]{0:T(1024)S(1)} %convert_element_type.38, f32[1536]{0:T(1024)S(1)} %add_rsqrt_fusion), kind=kLoop, calls=%fused_computation.18 | loop fusion | flops 6291456 | bytes 6301696 | tf_op jit(solution)/shard_map/convert_element_type | solution.py:27
  43.7 3.2 copy.91
  46.9 3.7 convolution_convert_fusion.1
  50.7 5.0 %copy.66 = bf16[8,1536,128]{1,0,2:T(8,128)(2,1)} copy(bf16[8,1536,128]{2,1,0:T(8,128)(2,1)} %convolution_convert_fusion.1) | data formatting | bytes 6291456 | tf_op jit(solution)/shard_map/convert_element_type | solution.py:31
  55.6 4.5 %all-to-all-start = ((bf16[8,1536,128]{1,0,2:T(8,128)(2,1)}), bf16[8,1536,128]{1,0,2:T(8,128)(2,1)}, u32[]{:S(2)}, u32[]{:S(2)}) async-start(bf16[8,1536,128]{1,0,2:T(8,128)(2,1)} %copy.66), calls=%async_computation | async-start | bytes 6291456 | tf_op jit(solution)/shard_map/all_to_all | solution.py:32
  60.1 4.6 %copy.74 = bf16[1536,1024]{0,1:T(8,128)(2,1)} copy(bf16[1536,1024]{1,0:T(8,128)(2,1)} %param.9) | data formatting | bytes 6291456 | tf_op args[4]
  64.8 5.3 %copy.75 = bf16[8,1536,128]{1,0,2:T(8,128)(2,1)} copy(bf16[8,1536,128]{1,2,0:T(8,128)(2,1)} %bitcast.97) | data formatting | bytes 6291456 | tf_op jit(solution)/shard_map/transpose | solution.py:38
  70.0 49.4 %all-to-all-done = bf16[8,1536,128]{1,0,2:T(8,128)(2,1)} async-done(((bf16[8,1536,128]{1,0,2:T(8,128)(2,1)}), bf16[8,1536,128]{1,0,2:T(8,128)(2,1)}, u32[]{:S(2)}, u32[]{:S(2)}) %all-to-all-start) | async-done | bytes 3145760 | tf_op jit(solution)/shard_map/all_to_all | solution.py:32
  119.5 15.5 %all-to-all-start.2 = ((bf16[8,1536,128]{1,0,2:T(8,128)(2,1)}), bf16[8,1536,128]{1,0,2:T(8,128)(2,1)}, u32[]{:S(2)}, u32[]{:S(2)}) async-start(bf16[8,1536,128]{1,0,2:T(8,128)(2,1)} %copy.75), calls=%async_computation.2 | async-start | bytes 6291456 | tf_op jit(solution)/shard_map/all_to_all | solution.py:39
  134.9 5.6 %convert_bitcast_fusion = f32[16,8,1536,8]{2,3,0,1:T(8,128)} fusion(bf16[8,1536,128]{1,0,2:T(8,128)(2,1)} %all-to-all-done), kind=kLoop, calls=%fused_computation.24 | loop fusion | flops 1572864 | bytes 9437184 | tf_op jit(solution)/shard_map/convert_element_type | solution.py:33
  140.5 53.8 %all-to-all-done.2 = bf16[8,1536,128]{1,0,2:T(8,128)(2,1)} async-done(((bf16[8,1536,128]{1,0,2:T(8,128)(2,1)}), bf16[8,1536,128]{1,0,2:T(8,128)(2,1)}, u32[]{:S(2)}, u32[]{:S(2)}) %all-to-all-start.2) | async-done | bytes 3145760 | tf_op jit(solution)/shard_map/all_to_all | solution.py:39
  194.3 0.0 copy-done
  194.3 8.4 %fusion.8 = bf16[128,1536,8]{1,0,2:T(8,128)(2,1)S(1)} fusion(f32[16,8,1536,8]{2,3,0,1:T(8,128)} %convert_bitcast_fusion, bf16[8,128,128]{2,1,0:T(8,128)(2,1)S(1)} %copy-done, bf16[16,8,1536,8]{2,1,3,0:T(8,128)(2,1)} %bitcast.13), kind=kOutput, calls=%fused_computation.15 | convolution fusion | flops 418381824 | bytes 12845056 | tf_op jit(solution)/shard_map/ctj,jbc->btj/dot_general | solution.py:42
  202.7 3.4 copy.78
  206.1 15.5 %all-to-all-start.3 = ((bf16[128,1536,8]{1,2,0:T(8,128)(2,1)}), bf16[128,1536,8]{1,2,0:T(8,128)(2,1)}, u32[]{:S(2)}, u32[]{:S(2)}) async-start(bf16[128,1536,8]{1,2,0:T(8,128)(2,1)} %copy.78), calls=%async_computation.3 | async-start | bytes 6291456 | tf_op jit(solution)/shard_map/all_to_all | solution.py:46
  221.6 16.2 %fusion.2 = bf16[128,1536,8]{1,0,2:T(8,128)(2,1)S(1)} fusion(f32[16,8,1536,8]{2,3,0,1:T(8,128)} %convert_bitcast_fusion), kind=kLoop, calls=%fused_computation.9 | loop fusion | flops 102236160 | bytes 9437184 | tf_op jit(solution)/shard_map/convert_element_type | solution.py:33
  237.8 0.0 copy-start.3
  237.8 1.7 copy-done.3
  239.5 2.8 convolution_convert_fusion
  242.3 5.0 %copy.70 = bf16[8,1536,128]{1,0,2:T(8,128)(2,1)} copy(bf16[8,1536,128]{2,1,0:T(8,128)(2,1)} %convolution_convert_fusion) | data formatting | bytes 6291456 | tf_op jit(solution)/shard_map/convert_element_type | solution.py:36
  247.2 0.0 copy-start.4
  247.2 33.8 %all-to-all-done.3 = bf16[128,1536,8]{1,2,0:T(8,128)(2,1)} async-done(((bf16[128,1536,8]{1,2,0:T(8,128)(2,1)}), bf16[128,1536,8]{1,2,0:T(8,128)(2,1)}, u32[]{:S(2)}, u32[]{:S(2)}) %all-to-all-start.3) | async-done | bytes 3145760 | tf_op jit(solution)/shard_map/all_to_all | solution.py:46
  281.0 15.5 %all-to-all-start.1 = ((bf16[8,1536,128]{1,0,2:T(8,128)(2,1)}), bf16[8,1536,128]{1,0,2:T(8,128)(2,1)}, u32[]{:S(2)}, u32[]{:S(2)}) async-start(bf16[8,1536,128]{1,0,2:T(8,128)(2,1)} %copy.70), calls=%async_computation.1 | async-start | bytes 6291456 | tf_op jit(solution)/shard_map/all_to_all | solution.py:37
  296.5 4.6 %fusion.35 = f32[8,128,128]{2,1,0:T(8,128)} fusion(bf16[128,1536,8]{1,0,2:T(8,128)(2,1)} %copy-done.3, bf16[16,8,1536,8]{2,1,3,0:T(8,128)(2,1)} %bitcast.13), kind=kOutput, calls=%fused_computation.54 | convolution fusion | flops 402653184 | bytes 6815744 | tf_op jit(solution)/shard_map/btj,ctj->jbc/dot_general | solution.py:41
  301.1 0.0 copy-done.4
  301.1 5.5 %fusion.33 = f32[8,1536,128]{1,2,0:T(8,128)} fusion(bf16[8,128,128]{2,1,0:T(8,128)(2,1)S(1)} %copy-done.4, bf16[8,1536,16,8]{1,3,0,2:T(8,128)(2,1)} %bitcast.17), kind=kOutput, calls=%fused_computation.52 | convolution fusion | flops 402653184 | bytes 9699328 | tf_op jit(solution)/shard_map/btj,bij->tbi/dot_general | solution.py:48
  306.6 3.7 fusion.31
  310.3 45.6 %all-to-all-done.1 = bf16[8,1536,128]{1,0,2:T(8,128)(2,1)} async-done(((bf16[8,1536,128]{1,0,2:T(8,128)(2,1)}), bf16[8,1536,128]{1,0,2:T(8,128)(2,1)}, u32[]{:S(2)}, u32[]{:S(2)}) %all-to-all-start.1) | async-done | bytes 3145760 | tf_op jit(solution)/shard_map/all_to_all | solution.py:37
  355.9 3.0 copy.72
  359.0 2.6 copy.73
  361.6 4.6 %copy.85 = bf16[1536,1024]{1,0:T(8,128)(2,1)} copy(bf16[1536,1024]{0,1:T(8,128)(2,1)} %bitcast.96) | data formatting | bytes 6291456
  366.2 0.0 copy-start.2
  366.2 6.7 %copy.81 = f32[1536,1024]{1,0:T(8,128)} copy(f32[1536,1024]{0,1:T(8,128)} %bitcast.92) | data formatting | bytes 12582912 | tf_op jit(solution)/shard_map/reshape | solution.py:50
  372.9 0.0 copy-done.2
  372.9 4.9 %fusion.16 = (f32[1024]{0:T(1024)}, f32[1536]{0:T(1024)S(1)}) fusion(f32[1536,1024]{1,0:T(8,128)} %copy.81, bf16[1536,1024]{1,0:T(8,128)(2,1)S(1)} %copy-done.2, f32[1536]{0:T(1024)S(1)} %add_rsqrt_fusion, f32[1024]{0:T(1024)S(1)} %convert_element_type.38), kind=kLoop, calls=%fused_computation.23 | loop fusion | flops 11007488 | bytes 9457664 | tf_op jit(solution)/shard_map/reduce_sum | solution.py:51
  377.8 43.9 %psum.15 = f32[1536]{0:T(1024)S(1)} all-reduce(f32[1536]{0:T(1024)S(1)} %get-tuple-element.21), channel_id=1, replica_groups=mesh['groups'=2,'blk'=16] {'blk'}, use_global_device_ids=true, to_apply=%region_3.0 | all-reduce | flops 1536 | bytes 12288 | tf_op jit(solution)/shard_map/psum | solution.py:53
  421.7 0.0 copy-start.1
  421.8 4.7 %fusion.14 = bf16[1536,1024]{1,0:T(8,128)(2,1)} fusion(bf16[1536,1024]{1,0:T(8,128)(2,1)S(1)} %copy-done.2, f32[1536,1024]{1,0:T(8,128)} %copy.81, f32[1536]{0:T(1024)S(1)} %fusion.43, f32[1024]{0:T(1024)S(1)} %convert_element_type.38, f32[1536]{0:T(1024)S(1)} %add_rsqrt_fusion), kind=kLoop, calls=%fused_computation.21 | loop fusion | flops 9437184 | bytes 12599296 | tf_op jit(solution)/shard_map/convert_element_type | solution.py:56
  426.4 0.0 copy-done.1
  (2 shorter events, 0.0 us)
Async XLA Ops:
  0.6 193.7 %copy-start = (bf16[8,128,128]{2,1,0:T(8,128)(2,1)S(1)}, bf16[8,128,128]{2,1,0:T(8,128)(2,1)}, u32[]{:S(2)}) copy-start(bf16[8,128,128]{2,1,0:T(8,128)(2,1)} %param.8) | copy-start | bytes 786436
  55.6 63.8 %all-to-all-start = ((bf16[8,1536,128]{1,0,2:T(8,128)(2,1)}), bf16[8,1536,128]{1,0,2:T(8,128)(2,1)}, u32[]{:S(2)}, u32[]{:S(2)}) async-start(bf16[8,1536,128]{1,0,2:T(8,128)(2,1)} %copy.66), calls=%async_computation | async-start | bytes 6291456 | tf_op jit(solution)/shard_map/all_to_all | solution.py:32
  119.5 74.9 %all-to-all-start.2 = ((bf16[8,1536,128]{1,0,2:T(8,128)(2,1)}), bf16[8,1536,128]{1,0,2:T(8,128)(2,1)}, u32[]{:S(2)}, u32[]{:S(2)}) async-start(bf16[8,1536,128]{1,0,2:T(8,128)(2,1)} %copy.75), calls=%async_computation.2 | async-start | bytes 6291456 | tf_op jit(solution)/shard_map/all_to_all | solution.py:39
  206.1 74.9 %all-to-all-start.3 = ((bf16[128,1536,8]{1,2,0:T(8,128)(2,1)}), bf16[128,1536,8]{1,2,0:T(8,128)(2,1)}, u32[]{:S(2)}, u32[]{:S(2)}) async-start(bf16[128,1536,8]{1,2,0:T(8,128)(2,1)} %copy.78), calls=%async_computation.3 | async-start | bytes 6291456 | tf_op jit(solution)/shard_map/all_to_all | solution.py:46
  237.8 1.7 copy-start.3
  247.2 53.9 %copy-start.4 = (bf16[8,128,128]{2,1,0:T(8,128)(2,1)S(1)}, bf16[8,128,128]{2,1,0:T(8,128)(2,1)}, u32[]{:S(2)}) copy-start(bf16[8,128,128]{2,1,0:T(8,128)(2,1)} %param.7) | copy-start | bytes 786436
  281.0 74.9 %all-to-all-start.1 = ((bf16[8,1536,128]{1,0,2:T(8,128)(2,1)}), bf16[8,1536,128]{1,0,2:T(8,128)(2,1)}, u32[]{:S(2)}, u32[]{:S(2)}) async-start(bf16[8,1536,128]{1,0,2:T(8,128)(2,1)} %copy.70), calls=%async_computation.1 | async-start | bytes 6291456 | tf_op jit(solution)/shard_map/all_to_all | solution.py:37
  366.2 6.7 %copy-start.2 = (bf16[1536,1024]{1,0:T(8,128)(2,1)S(1)}, bf16[1536,1024]{1,0:T(8,128)(2,1)}, u32[]{:S(2)}) copy-start(bf16[1536,1024]{1,0:T(8,128)(2,1)} %param.5) | copy-start | bytes 9437188
  421.7 4.7 %copy-start.1 = (bf16[8,128,128]{2,1,0:T(8,128)(2,1)S(1)}, bf16[8,128,128]{2,1,0:T(8,128)(2,1)}, u32[]{:S(2)}) copy-start(bf16[8,128,128]{2,1,0:T(8,128)(2,1)} %param.8) | copy-start | bytes 786436
where the time goes:
time: 428 us; the launch traced here: 426 us
  waiting for transfers between devices  183 us (43%)
  blocking collectives  79.4 us (19%)
  starting transfers between devices  50.9 us (12%)
  local copies, waits for them, and re-layouts  45 us (11%)
  other arithmetic  39 us (9%)
  matrix products  28.7 us (7%)
    all_to_all x1, waiting for transfers between devices, on_device(): lax.all_to_all(incoming, 'blk', split_axis=2, concat_axis=0, tiled=True)  53.8 us
    all_to_all x1, waiting for transfers between devices, on_device(): lax.all_to_all(pre_act, 'blk', split_axis=2, concat_axis=0, tiled=True)  49.4 us
    all_to_all x1, waiting for transfers between devices, on_device(): lax.all_to_all(mixed_out, 'blk', split_axis=2, concat_axis=0, tiled=True)  45.6 us
    psum x1, blocking collectives, on_device(): correction = lax.psum(jnp.sum(scaled * widened, axis=1), 'blk')  43.9 us
    psum x1, blocking collectives, on_device(): square_sum = lax.psum(jnp.sum(widened * widened, axis=1), 'blk')  35.4 us
    all_to_all x1, waiting for transfers between devices, on_device(): lax.all_to_all(grad_pre, 'blk', split_axis=0, concat_axis=2, tiled=True)  33.8 us
    convert_element_type x1, other arithmetic, on_device(): jax.nn.gelu(pre_piece.astype(jnp.float32), approximate=False)  16.2 us
    all_to_all x1, starting transfers between devices, on_device(): lax.all_to_all(mixed_out, 'blk', split_axis=2, concat_axis=0, tiled=True)  15.5 us
  transfers between devices with their start and end apart: 4, of which 4 were waited for; matrix products, arithmetic and copies ran while one was open for 12% of the time, Pallas kernels for 0%

commit v1 on v0

--- a/solution.py
+++ b/solution.py
@@ -1,9 +1,11 @@
 import jax
 import jax.numpy as jnp
 from jax import lax
+from jax.experimental import pallas as pl
+from jax.experimental.pallas import tpu as pltpu
 from jax.sharding import PartitionSpec as P
 
-D = 16384
+CHUNK = 256
 
 
 epsilon = 1e-06
@@ -16,13 +18,13 @@
     )
 
 
-def on_device(tokens, norm_gain, left_factor, right_factor, cotangent):
+def on_device(width, tokens, norm_gain, left_factor, right_factor, cotangent):
     row_count = tokens.shape[0]
     local_blocks = left_factor.shape[0]
     block_order = left_factor.shape[1]
     widened = tokens.astype(jnp.float32)
     square_sum = lax.psum(jnp.sum(widened * widened, axis=1), "blk")
-    inverse_rms = lax.rsqrt(square_sum / D + epsilon)
+    inverse_rms = lax.rsqrt(square_sum / width + epsilon)
     gain_wide = norm_gain.astype(jnp.float32)
     normed = (widened * inverse_rms[:, None] * gain_wide[None, :]).astype(jnp.bfloat16)
     blocks = normed.reshape(row_count, local_blocks, block_order)
@@ -52,9 +54,376 @@
     scaled = grad_normed * gain_wide[None, :]
     correction = lax.psum(jnp.sum(scaled * widened, axis=1), "blk")
     grad_tokens = (
-        inverse_rms[:, None] * scaled - widened * (inverse_rms**3 * correction / D)[:, None]
+        inverse_rms[:, None] * scaled - widened * (inverse_rms**3 * correction / width)[:, None]
     ).astype(jnp.bfloat16)
     return (mixer_out, grad_tokens, grad_left, grad_right, grad_gain)
+
+def fast(n, width, tokens, norm_gain, left_factor, right_factor, cotangent):
+    rows = tokens.shape[0]
+    feats = tokens.shape[1]
+    local, order = left_factor.shape[0], left_factor.shape[1]
+    piece = local * local
+    lg = local.bit_length() - 1
+    low = local - 1
+    tc = CHUNK
+    chunks = rows // tc
+    strips = rows // 128
+    f32, bf16 = jnp.float32, jnp.bfloat16
+    part = 256
+    pieces_in_part = part // piece
+
+    def nn(a, b):
+        return lax.dot_general(a, b, (((1,), (0,)), ((), ())), preferred_element_type=f32)
+
+    def nt(a, b):
+        return lax.dot_general(a, b, (((1,), (1,)), ((), ())), preferred_element_type=f32)
+
+    def tn(a, b):
+        return lax.dot_general(a, b, (((0,), (0,)), ((), ())), preferred_element_type=f32)
+
+    def to_row(column):
+        return jnp.transpose(jnp.broadcast_to(column, (128, 128)))[0:1, :]
+
+    def to_lanes(row):
+        return jnp.transpose(jnp.broadcast_to(row, (128, 128)))
+
+    def kernel(
+        tok, gain, left, right, cot,
+        mixer, gtok, gleft, gright, ggain,
+        send_a, send_b, cot_in, pre_in, gp_in, mix_in,
+        perm, regroup, back_w, fwd_w,
+        flat, act, slope, act_q, gm_q, gn,
+        inv, corr, stat_out, stat_in, corr_out, corr_in,
+        ssem, rsem, stat_ssem, stat_rsem,
+    ):
+        me = lax.axis_index("blk")
+
+        def peer(i):
+            off = n // 2 + i
+            off = off + off // n
+            return lax.rem(me + off, n)
+
+        barrier = pltpu.get_barrier_semaphore()
+
+        def greet(i, c):
+            pl.semaphore_signal(barrier, inc=1, device_id={"blk": peer(i)})
+            return c
+
+        lax.fori_loop(0, n - 1, greet, 0)
+
+        def fill(ref, count, test):
+            def body(i, c):
+                r = lax.broadcasted_iota(jnp.int32, (128, ref.shape[1]), 0) + i * 128
+                q = lax.broadcasted_iota(jnp.int32, (128, ref.shape[1]), 1)
+                ref[pl.ds(pl.multiple_of(i * 128, 128), 128), :] = jnp.where(test(r, q), 1.0, 0.0).astype(bf16)
+                return c
+
+            lax.fori_loop(0, count // 128, body, 0)
+
+        def push(out, into, which, k):
+            def body(i, c):
+                to = peer(i)
+                pltpu.make_async_remote_copy(
+                    src_ref=out.at[k, to],
+                    dst_ref=into.at[k, me],
+                    send_sem=ssem.at[which, k],
+                    recv_sem=rsem.at[which, k],
+                    device_id={"blk": to},
+                ).start()
+                return c
+
+            lax.fori_loop(0, n - 1, body, 0)
+
+        def landed(into, which, k):
+            span = into.at[k, pl.ds(0, n - 1)]
+            pltpu.make_async_copy(span, span, rsem.at[which, k]).wait()
+
+        def sent(out, which, k):
+            span = out.at[k, pl.ds(0, n - 1)]
+            pltpu.make_async_copy(span, span, ssem.at[which, k]).wait()
+
+        def push_stat(out, into, which):
+            def body(i, c):
+                pltpu.make_async_remote_copy(
+                    src_ref=out,
+                    dst_ref=into.at[me],
+                    send_sem=stat_ssem.at[which],
+                    recv_sem=stat_rsem.at[which],
+                    device_id={"blk": peer(i)},
+                ).start()
+                return c
+
+            into[me] = out[...]
+            lax.fori_loop(0, n - 1, body, 0)
+
+        def stat_landed(into, which):
+            span = into.at[pl.ds(0, n - 1)]
+            pltpu.make_async_copy(span, span, stat_rsem.at[which]).wait()
+
+        def stat_sent(into, which):
+            span = into.at[pl.ds(0, n - 1)]
+            pltpu.make_async_copy(span, span, stat_ssem.at[which]).wait()
+
+        def rows_of(k):
+            return pl.ds(pl.multiple_of(k * tc, tc), tc)
+
+        def put(out, into, k, i, value):
+            out[k, pl.ds(i * pieces_in_part, pieces_in_part)] = value.astype(bf16).reshape(
+                pieces_in_part, piece, tc
+            )
+
+        def scatter(natural, out, into, k):
+            def body(i, c):
+                block = perm[pl.ds(pl.multiple_of(i * part, part), part), :]
+                put(out, into, k, i, nt(block, natural()))
+                return c
+
+            lax.fori_loop(0, feats // part, body, 0)
+
+        def own(out, into, k):
+            into[k, me] = out[k, me]
+
+        fill(perm, feats, lambda r, q: q == (r & low) * order + (r >> lg))
+
+        stat_out[...] = jnp.zeros_like(stat_out)
+        for s in range(strips):
+            x = tok[s * 128 : (s + 1) * 128, :].astype(f32)
+            stat_out[s : s + 1, :] = to_row(jnp.sum(x * x, axis=1, keepdims=True))
+        pl.semaphore_wait(barrier, n - 1)
+        push_stat(stat_out, stat_in, 0)
+
+        def cot_step(k, c):
+            scatter(lambda: cot[rows_of(k), :], send_a, cot_in, k)
+            push(send_a, cot_in, 0, k)
+            own(send_a, cot_in, k)
+            return c
+
+        lax.fori_loop(0, chunks, cot_step, 0)
+
+        stat_landed(stat_in, 0)
+        total = jnp.sum(stat_in[...], axis=0)
+        for s in range(strips):
+            inv[s * 128 : (s + 1) * 128, :] = lax.rsqrt(to_lanes(total[s : s + 1, :]) / width + epsilon)
+
+        def normed_block(k, b):
+            cols = pl.ds(pl.multiple_of(b * order, order), order)
+            x = tok[rows_of(k), cols].astype(f32)
+            return (x * inv[rows_of(k), :] * gain[:, cols]).astype(bf16)
+
+        def pre_step(k, c):
+            def body(b, c):
+                cols = pl.ds(pl.multiple_of(b * order, order), order)
+                flat[:, cols] = nn(normed_block(k, b), left[b]).astype(bf16)
+                return c
+
+            lax.fori_loop(0, local, body, 0)
+            scatter(lambda: flat[...], send_b, pre_in, k)
+            push(send_b, pre_in, 1, k)
+            own(send_b, pre_in, k)
+            return c
+
+        lax.fori_loop(0, chunks, pre_step, 0)
+
+        fill(
+            regroup,
+            feats,
+            lambda q, r: q == ((r >> lg) & low) * order + (r >> (2 * lg)) * local + (r & low),
+        )
+
+        def expand_step(i, c):
+            rs = pl.ds(pl.multiple_of(i * 128, 128), 128)
+            r = lax.broadcasted_iota(jnp.int32, (128, order), 0) + i * 128
+            y = lax.broadcasted_iota(jnp.int32, (128, order), 1)
+            pick = jnp.where(y == (r >> (2 * lg)) * local + (r & low), 1.0, 0.0).astype(bf16)
+            for j in range(local):
+                cols = slice(j * order, (j + 1) * order)
+                here = ((r >> lg) & low) == j
+                back_w[rs, cols] = jnp.where(here, nn(pick, right[j]), 0.0).astype(bf16)
+                fwd_w[rs, cols] = jnp.where(here, nt(pick, right[j]), 0.0).astype(bf16)
+            return c
+
+        lax.fori_loop(0, feats // 128, expand_step, 0)
+        gleft[...] = jnp.zeros_like(gleft)
+        gright[...] = jnp.zeros_like(gright)
+        ggain[...] = jnp.zeros_like(ggain)
+
+        def middle_step(k, c):
+            landed(cot_in, 0, k)
+            landed(pre_in, 1, k)
+
+            def gelu(i, c):
+                rs = pl.ds(pl.multiple_of(i * part, part), part)
+                v = pre_in[k, pl.ds(i * pieces_in_part, pieces_in_part)].reshape(part, tc).astype(f32)
+                half = 0.5 * (1.0 + lax.erf(v * 0.7071067811865476))
+                act[rs, :] = (v * half).astype(bf16)
+                slope[rs, :] = half + v * jnp.exp(-0.5 * v * v) * 0.3989422804014327
+                return c
+
+            lax.fori_loop(0, feats // part, gelu, 0)
+
+            def group(i, c):
+                rs = pl.ds(pl.multiple_of(i * part, part), part)
+                block = regroup[rs, :]
+                act_q[rs, :] = nn(block, act[...]).astype(bf16)
+                gm_q[rs, :] = nn(block, cot_in[k].reshape(feats, tc)).astype(bf16)
+                return c
+
+            lax.fori_loop(0, feats // part, group, 0)
+            sent(send_b, 1, k)
+
+            def grad(i, c):
+                rs = pl.ds(pl.multiple_of(i * part, part), part)
+                put(send_b, gp_in, k, i, nn(back_w[rs, :], gm_q[...]) * slope[rs, :])
+                return c
+
+            lax.fori_loop(0, feats // part, grad, 0)
+            push(send_b, gp_in, 2, k)
+            own(send_b, gp_in, k)
+            sent(send_a, 0, k)
+
+            def mix(i, c):
+                rs = pl.ds(pl.multiple_of(i * part, part), part)
+                put(send_a, mix_in, k, i, nn(fwd_w[rs, :], act_q[...]))
+                return c
+
+            lax.fori_loop(0, feats // part, mix, 0)
+            push(send_a, mix_in, 3, k)
+            own(send_a, mix_in, k)
+
+            def factor(j, c):
+                rs = pl.ds(pl.multiple_of(j * order, order), order)
+                gright[j] += nt(act_q[rs, :], gm_q[rs, :])
+                return c
+
+            lax.fori_loop(0, local, factor, 0)
+            return c
+
+        lax.fori_loop(0, chunks, middle_step, 0)
+
+        corr_out[...] = jnp.zeros_like(corr_out)
+
+        def turn(into, k):
+            for s in range(tc // 128):
+                flat[s * 128 : (s + 1) * 128, :] = jnp.transpose(
+                    into[k, :, :, s * 128 : (s + 1) * 128].reshape(feats, 128)
+                )
+
+        def last_step(k, c):
+            landed(gp_in, 2, k)
+            turn(gp_in, k)
+
+            def body(b, total):
+                cols = pl.ds(pl.multiple_of(b * order, order), order)
+                g = nn(flat[...], perm[:, cols]).astype(bf16)
+                grad = nt(g, left[b])
+                gn[rows_of(k), cols] = grad
+                gleft[b] += tn(normed_block(k, b), g)
+                x = tok[rows_of(k), cols].astype(f32)
+                gx = grad * x
+                ggain[:, cols] += jnp.sum(gx * inv[rows_of(k), :], axis=0, keepdims=True)
+                return total + gx * gain[:, cols]
+
+            corr[rows_of(k), :] = lax.fori_loop(0, local, body, jnp.zeros((tc, order), f32))
+            return c
+
+        lax.fori_loop(0, chunks, last_step, 0)
+        for s in range(strips):
+            corr_out[s : s + 1, :] = to_row(
+                jnp.sum(corr[s * 128 : (s + 1) * 128, :], axis=1, keepdims=True)
+            )
+        push_stat(corr_out, corr_in, 1)
+
+        def out_step(k, c):
+            landed(mix_in, 3, k)
+            turn(mix_in, k)
+
+            def body(b, c):
+                cols = pl.ds(pl.multiple_of(b * part, part), part)
+                mixer[rows_of(k), cols] = nn(flat[...], perm[:, cols]).astype(bf16)
+                return c
+
+            lax.fori_loop(0, feats // part, body, 0)
+            return c
+
+        early = max(chunks - 2, 0)
+        lax.fori_loop(0, early, out_step, 0)
+
+        stat_landed(corr_in, 1)
+        total = jnp.sum(corr_in[...], axis=0)
+        for s in range(strips):
+            rs = slice(s * 128, (s + 1) * 128)
+            r = inv[rs, :]
+            corr[rs, :] = r * r * r * to_lanes(total[s : s + 1, :]) / width
+
+        def token_step(k, c):
+            def body(b, c):
+                cols = pl.ds(pl.multiple_of(b * order, order), order)
+                x = tok[rows_of(k), cols].astype(f32)
+                scaled = gn[rows_of(k), cols] * gain[:, cols]
+                gtok[rows_of(k), cols] = (
+                    inv[rows_of(k), :] * scaled - x * corr[rows_of(k), :]
+                ).astype(bf16)
+                return c
+
+            lax.fori_loop(0, local, body, 0)
+            return c
+
+        lax.fori_loop(0, chunks, token_step, 0)
+        lax.fori_loop(early, chunks, out_step, 0)
+
+        def drain(k, c):
+            sent(send_b, 2, k)
+            sent(send_a, 3, k)
+            return c
+
+        lax.fori_loop(0, chunks, drain, 0)
+        stat_sent(stat_in, 0)
+        stat_sent(corr_in, 1)
+
+    exchange = pltpu.VMEM((chunks, n, piece, tc), bf16)
+    square = pltpu.VMEM((feats, feats), bf16)
+    stat_rows = -(-strips // 8) * 8
+    vmem = pl.BlockSpec(memory_space=pltpu.VMEM)
+    outs = pl.pallas_call(
+        kernel,
+        out_shape=(
+            jax.ShapeDtypeStruct((rows, feats), bf16),
+            jax.ShapeDtypeStruct((rows, feats), bf16),
+            jax.ShapeDtypeStruct((local, order, order), f32),
+            jax.ShapeDtypeStruct((local, order, order), f32),
+            jax.ShapeDtypeStruct((1, feats), f32),
+        ),
+        in_specs=[vmem] * 5,
+        out_specs=(vmem,) * 5,
+        scratch_shapes=[exchange] * 6
+        + [square] * 4
+        + [
+            pltpu.VMEM((tc, feats), bf16),
+            pltpu.VMEM((feats, tc), bf16),
+            pltpu.VMEM((feats, tc), f32),
+            pltpu.VMEM((feats, tc), bf16),
+            pltpu.VMEM((feats, tc), bf16),
+            pltpu.VMEM((rows, feats), f32),
+            pltpu.VMEM((rows, 128), f32),
+            pltpu.VMEM((rows, 128), f32),
+            pltpu.VMEM((stat_rows, 128), f32),
+            pltpu.VMEM((n, stat_rows, 128), f32),
+            pltpu.VMEM((stat_rows, 128), f32),
+            pltpu.VMEM((n, stat_rows, 128), f32),
+            pltpu.SemaphoreType.DMA((4, chunks)),
+            pltpu.SemaphoreType.DMA((4, chunks)),
+            pltpu.SemaphoreType.DMA((2,)),
+            pltpu.SemaphoreType.DMA((2,)),
+        ],
+        compiler_params=pltpu.CompilerParams(
+            collective_id=0, has_side_effects=True, vmem_limit_bytes=60 * 1024 * 1024
+        ),
+        cost_estimate=pl.CostEstimate(
+            flops=20 * rows * feats * feats, bytes_accessed=8 * rows * feats, transcendentals=2 * rows * feats
+        ),
+        name="monarch",
+    )(tokens, norm_gain.astype(f32).reshape(1, feats), left_factor, right_factor, cotangent)
+    return (*outs[:4], outs[4].reshape(feats))
 
 
 def solution(mesh):
@@ -65,8 +434,28 @@
         P("blk", None, None),
         P("groups", "blk"),
     )
+    n = mesh.shape["blk"]
+
+    def body(tokens, norm_gain, left_factor, right_factor, cotangent):
+        rows, feats = tokens.shape
+        local, order = left_factor.shape[0], left_factor.shape[1]
+        fits = (
+            n > 1
+            and local & (local - 1) == 0
+            and (local * local) % 16 == 0
+            and 256 % (local * local) == 0
+            and order == 128
+            and n * local == order
+            and right_factor.shape == left_factor.shape
+            and rows % CHUNK == 0
+            and feats % 256 == 0
+        )
+        if fits:
+            return fast(n, n * feats, tokens, norm_gain, left_factor, right_factor, cotangent)
+        return on_device(n * feats, tokens, norm_gain, left_factor, right_factor, cotangent)
+
     return jax.shard_map(
-        on_device,
+        body,
         mesh=mesh,
         in_specs=placed,
         out_specs=(

time: 428 us -> 307 us (0.72)
  Pallas kernels: 0 us -> 297 us
  waiting for transfers between devices: 183 us -> 0 us
  blocking collectives: 79.4 us -> 0 us
  starting transfers between devices: 50.9 us -> 0 us
  other arithmetic: 39 us -> 1.28 us
  local copies, waits for them, and re-layouts: 45 us -> 7.88 us
  matrix products: 28.7 us -> 0 us
    pallas_call x0 -> x1, Pallas kernels: none -> 297 us  [fast(): pl.pallas_call(kernel, out_shape=(jax.ShapeDtypeStruct((rows, feats), bf1...]
    all_to_all x4 -> x0, waiting for transfers between devices: 183 us -> none  [the longest x1 53.8 us: on_device(): lax.all_to_all(incoming, 'blk', split_axis=2, concat_axis=0, tiled=True)]
    psum x2 -> x0, blocking collectives: 79.4 us -> none  [the longest x1 43.9 us: on_device(): correction = lax.psum(jnp.sum(scaled * widened, axis=1), 'blk')]
    all_to_all x4 -> x0, starting transfers between devices: 50.9 us -> none  [the longest x1 15.5 us: on_device(): lax.all_to_all(mixed_out, 'blk', split_axis=2, concat_axis=0, tiled=True)]
    convert_element_type x5 -> x0, other arithmetic: 31.5 us -> none  [the longest x1 16.2 us: on_device(): jax.nn.gelu(pre_piece.astype(jnp.float32), approximate=False)]
    dot_general x6 -> x0, matrix products: 28.7 us -> none  [the longest x1 8.36 us: on_device(): jnp.einsum('ctj,jbc->btj', grad_mixed, right_factor, preferred_element_ty...]
    convert_element_type x3 -> x0, local copies, waits for them, and re-layouts: 13.3 us -> none  [the longest x1 4.96 us: on_device(): pre_act = jnp.einsum('tbi,bij->btj', blocks, left_factor, preferred_eleme...]
    reshape x2 -> x0, local copies, waits for them, and re-layouts: 9.85 us -> none  [the longest x1 6.68 us: on_device(): grad_normed = jnp.einsum('btj,bij->tbi', grad_back, left_factor, preferre...]
  transfers between devices with their start and end apart: 4 -> 0, of which waited for: 4 -> 0; matrix products, arithmetic and copies ran while one was open for 12% -> 0% of each run, Pallas kernels for 0% -> 0%
where the time goes in v1:
time: 307 us
  Pallas kernels  297 us (97%)
  local copies, waits for them, and re-layouts  7.88 us (3%)
    pallas_call x1, Pallas kernels, fast(): pl.pallas_call(kernel, out_shape=(jax.ShapeDtypeStruct((rows, feats), bf1...  297 us
    unnamed x13, local copies, waits for them, and re-layouts  7.88 us

profile of v1, /device:TPU:0, one launch (start us, length us, event | category | flops | bytes accessed | tf_op | source)
XLA Modules:
  0.0 307.0 jit_solution(933539871012263705)
XLA Ops:
  0.6 1.3 reshape.21
  1.9 297.2 %monarch.1 = (bf16[1536,1024]{1,0:T(8,128)(2,1)}, bf16[1536,1024]{1,0:T(8,128)(2,1)}, f32[8,128,128]{2,1,0:T(8,128)}, f32[8,128,128]{2,1,0:T(8,128)}, f32[1,1024]{1,0:T(1,128)}) custom-call(bf16[1536,1024]{1,0:T(8,128)(2,1)} %tok.1, f32[1,1024]{1,0:T(1,128)} %bitcast.2, bf16[8,128,128]{2,1,0:T(8,128)(2,1)} %left.1, bf16[8,128,128]{2,1,0:T(8,128)(2,1)} %right.1, ...), custom_call_target="tpu_custom_call" | custom-call | flops 32212254720 | bytes 12582912 | tf_op jit(solution)/shard_map/monarch/pallas_call | solution.py:387
  299.1 0.0 copy-start
  299.1 4.0 %copy.15 = bf16[1536,1024]{1,0:T(8,128)(2,1)} copy(bf16[1536,1024]{1,0:T(8,128)(2,1)} %get-tuple-element.20) | data formatting | bytes 6291456
  303.1 0.0 copy-done
  303.1 0.0 copy-start.2
  303.1 0.0 copy-start.1
  303.1 0.0 copy-start.3
  303.1 1.7 copy.16
  304.8 0.0 copy-done.2
  304.8 0.8 copy.17
  305.6 0.0 copy-done.1
  305.6 0.8 copy.18
  306.4 0.0 copy-done.3
  306.4 0.6 copy.19
Async XLA Ops:
  299.1 4.0 %copy-start = (bf16[1536,1024]{1,0:T(8,128)(2,1)S(1)}, bf16[1536,1024]{1,0:T(8,128)(2,1)}, u32[]{:S(2)}) copy-start(bf16[1536,1024]{1,0:T(8,128)(2,1)} %get-tuple-element.21) | copy-start | bytes 9437188
  303.1 1.7 copy-start.2
  303.1 2.5 copy-start.1
  303.1 3.3 %copy-start.3 = (f32[1,1024]{1,0:T(1,128)S(1)}, f32[1,1024]{1,0:T(1,128)}, u32[]{:S(2)}) copy-start(f32[1,1024]{1,0:T(1,128)} %get-tuple-element.14) | copy-start | bytes 12292

commit v2 on v1

--- a/solution.py
+++ b/solution.py
@@ -58,6 +58,44 @@
     ).astype(jnp.bfloat16)
     return (mixer_out, grad_tokens, grad_left, grad_right, grad_gain)
 
+def hand_over(arrays, pieces):
+    count = len(arrays)
+
+    def kernel(*refs):
+        held, taken, given = refs[2 * count : 3 * count], refs[-2], refs[-1]
+        copies = []
+        for i in range(count):
+            rows = arrays[i].shape[0]
+            parts = pieces if rows % (pieces * 16) == 0 else 1
+            step = rows // parts
+            for p in range(parts):
+                span = pl.ds(p * step, step)
+                inward = pltpu.make_async_copy(refs[i].at[span], held[i].at[span], taken.at[i, p])
+                outward = pltpu.make_async_copy(
+                    held[i].at[span], refs[count + i].at[span], given.at[i, p]
+                )
+                copies.append((inward, outward))
+        for inward, outward in copies:
+            inward.start()
+        for inward, outward in copies:
+            inward.wait()
+            outward.start()
+        for inward, outward in copies:
+            outward.wait()
+
+    anywhere = pl.BlockSpec(memory_space=pl.ANY)
+    return pl.pallas_call(
+        kernel,
+        out_shape=tuple(jax.ShapeDtypeStruct(a.shape, a.dtype) for a in arrays),
+        in_specs=[anywhere] * count,
+        out_specs=(anywhere,) * count,
+        scratch_shapes=[pltpu.VMEM(a.shape, a.dtype) for a in arrays]
+        + [pltpu.SemaphoreType.DMA((count, pieces))] * 2,
+        compiler_params=pltpu.CompilerParams(vmem_limit_bytes=60 * 1024 * 1024),
+        name="hand_over",
+    )(*arrays)
+
+
 def fast(n, width, tokens, norm_gain, left_factor, right_factor, cotangent):
     rows = tokens.shape[0]
     feats = tokens.shape[1]
@@ -88,15 +126,19 @@
         return jnp.transpose(jnp.broadcast_to(row, (128, 128)))
 
     def kernel(
-        tok, gain, left, right, cot,
-        mixer, gtok, gleft, gright, ggain,
+        tok_hbm, gain, left, right, cot_hbm,
+        mixer_hbm, gtok_hbm, gleft_hbm, gright_hbm, ggain,
+        tok, cot, gleft, gright,
         send_a, send_b, cot_in, pre_in, gp_in, mix_in,
         perm, regroup, back_w, fwd_w,
         flat, act, slope, act_q, gm_q, gn,
         inv, corr, stat_out, stat_in, corr_out, corr_in,
-        ssem, rsem, stat_ssem, stat_rsem,
+        ssem, rsem, stat_ssem, stat_rsem, load_sem, tok_sem, mix_sem, gtok_sem, grad_sem,
     ):
         me = lax.axis_index("blk")
+
+        def rows_of(k):
+            return pl.ds(pl.multiple_of(k * tc, tc), tc)
 
         def peer(i):
             off = n // 2 + i
@@ -110,6 +152,17 @@
             return c
 
         lax.fori_loop(0, n - 1, greet, 0)
+
+        def load(k):
+            return pltpu.make_async_copy(cot_hbm.at[rows_of(k)], cot.at[rows_of(k)], load_sem.at[k])
+
+        def load_start(k, c):
+            load(k).start()
+            return c
+
+        lax.fori_loop(0, chunks, load_start, 0)
+        load_tok = pltpu.make_async_copy(tok_hbm, tok, tok_sem)
+        load_tok.start()
 
         def fill(ref, count, test):
             def body(i, c):
@@ -164,9 +217,6 @@
             span = into.at[pl.ds(0, n - 1)]
             pltpu.make_async_copy(span, span, stat_ssem.at[which]).wait()
 
-        def rows_of(k):
-            return pl.ds(pl.multiple_of(k * tc, tc), tc)
-
         def put(out, into, k, i, value):
             out[k, pl.ds(i * pieces_in_part, pieces_in_part)] = value.astype(bf16).reshape(
                 pieces_in_part, piece, tc
@@ -185,20 +235,23 @@
 
         fill(perm, feats, lambda r, q: q == (r & low) * order + (r >> lg))
 
+        def cot_step(k, c):
+            load(k).wait()
+            scatter(lambda: cot[rows_of(k), :], send_a, cot_in, k)
+            push(send_a, cot_in, 0, k)
+            own(send_a, cot_in, k)
+            return c
+
+        pl.semaphore_wait(barrier, n - 1)
+        cot_step(0, 0)
+        load_tok.wait()
         stat_out[...] = jnp.zeros_like(stat_out)
         for s in range(strips):
             x = tok[s * 128 : (s + 1) * 128, :].astype(f32)
             stat_out[s : s + 1, :] = to_row(jnp.sum(x * x, axis=1, keepdims=True))
-        pl.semaphore_wait(barrier, n - 1)
         push_stat(stat_out, stat_in, 0)
 
-        def cot_step(k, c):
-            scatter(lambda: cot[rows_of(k), :], send_a, cot_in, k)
-            push(send_a, cot_in, 0, k)
-            own(send_a, cot_in, k)
-            return c
-
-        lax.fori_loop(0, chunks, cot_step, 0)
+        lax.fori_loop(1, chunks, cot_step, 0)
 
         stat_landed(stat_in, 0)
         total = jnp.sum(stat_in[...], axis=0)
@@ -287,7 +340,6 @@
                 return c
 
             lax.fori_loop(0, feats // part, mix, 0)
-            push(send_a, mix_in, 3, k)
             own(send_a, mix_in, k)
 
             def factor(j, c):
@@ -299,6 +351,15 @@
             return c
 
         lax.fori_loop(0, chunks, middle_step, 0)
+        copy_right = pltpu.make_async_copy(gright, gright_hbm, grad_sem.at[1])
+        copy_right.start()
+        early = max(chunks - 2, 0)
+
+        def push_mix(k, c):
+            push(send_a, mix_in, 3, k)
+            return c
+
+        lax.fori_loop(0, early, push_mix, 0)
 
         corr_out[...] = jnp.zeros_like(corr_out)
 
@@ -332,6 +393,15 @@
                 jnp.sum(corr[s * 128 : (s + 1) * 128, :], axis=1, keepdims=True)
             )
         push_stat(corr_out, corr_in, 1)
+        lax.fori_loop(early, chunks, push_mix, 0)
+        copy_left = pltpu.make_async_copy(gleft, gleft_hbm, grad_sem.at[0])
+        copy_left.start()
+
+        def store_mix(k):
+            return pltpu.make_async_copy(cot.at[rows_of(k)], mixer_hbm.at[rows_of(k)], mix_sem.at[k])
+
+        def store_tok(k):
+            return pltpu.make_async_copy(tok.at[rows_of(k)], gtok_hbm.at[rows_of(k)], gtok_sem.at[k])
 
         def out_step(k, c):
             landed(mix_in, 3, k)
@@ -339,13 +409,13 @@
 
             def body(b, c):
                 cols = pl.ds(pl.multiple_of(b * part, part), part)
-                mixer[rows_of(k), cols] = nn(flat[...], perm[:, cols]).astype(bf16)
+                cot[rows_of(k), cols] = nn(flat[...], perm[:, cols]).astype(bf16)
                 return c
 
             lax.fori_loop(0, feats // part, body, 0)
-            return c
-
-        early = max(chunks - 2, 0)
+            store_mix(k).start()
+            return c
+
         lax.fori_loop(0, early, out_step, 0)
 
         stat_landed(corr_in, 1)
@@ -360,12 +430,13 @@
                 cols = pl.ds(pl.multiple_of(b * order, order), order)
                 x = tok[rows_of(k), cols].astype(f32)
                 scaled = gn[rows_of(k), cols] * gain[:, cols]
-                gtok[rows_of(k), cols] = (
+                tok[rows_of(k), cols] = (
                     inv[rows_of(k), :] * scaled - x * corr[rows_of(k), :]
                 ).astype(bf16)
                 return c
 
             lax.fori_loop(0, local, body, 0)
+            store_tok(k).start()
             return c
 
         lax.fori_loop(0, chunks, token_step, 0)
@@ -374,16 +445,21 @@
         def drain(k, c):
             sent(send_b, 2, k)
             sent(send_a, 3, k)
+            store_mix(k).wait()
+            store_tok(k).wait()
             return c
 
         lax.fori_loop(0, chunks, drain, 0)
         stat_sent(stat_in, 0)
         stat_sent(corr_in, 1)
+        copy_left.wait()
+        copy_right.wait()
 
     exchange = pltpu.VMEM((chunks, n, piece, tc), bf16)
     square = pltpu.VMEM((feats, feats), bf16)
     stat_rows = -(-strips // 8) * 8
     vmem = pl.BlockSpec(memory_space=pltpu.VMEM)
+    anywhere = pl.BlockSpec(memory_space=pl.ANY)
     outs = pl.pallas_call(
         kernel,
         out_shape=(
@@ -393,9 +469,11 @@
             jax.ShapeDtypeStruct((local, order, order), f32),
             jax.ShapeDtypeStruct((1, feats), f32),
         ),
-        in_specs=[vmem] * 5,
-        out_specs=(vmem,) * 5,
-        scratch_shapes=[exchange] * 6
+        in_specs=[anywhere, vmem, vmem, vmem, anywhere],
+        out_specs=(anywhere,) * 4 + (vmem,),
+        scratch_shapes=[pltpu.VMEM((rows, feats), bf16)] * 2
+        + [pltpu.VMEM((local, order, order), f32)] * 2
+        + [exchange] * 6
         + [square] * 4
         + [
             pltpu.VMEM((tc, feats), bf16),
@@ -414,6 +492,11 @@
             pltpu.SemaphoreType.DMA((4, chunks)),
             pltpu.SemaphoreType.DMA((2,)),
             pltpu.SemaphoreType.DMA((2,)),
+            pltpu.SemaphoreType.DMA((chunks,)),
+            pltpu.SemaphoreType.DMA,
+            pltpu.SemaphoreType.DMA((chunks,)),
+            pltpu.SemaphoreType.DMA((chunks,)),
+            pltpu.SemaphoreType.DMA((2,)),
         ],
         compiler_params=pltpu.CompilerParams(
             collective_id=0, has_side_effects=True, vmem_limit_bytes=60 * 1024 * 1024
@@ -423,6 +506,7 @@
         ),
         name="monarch",
     )(tokens, norm_gain.astype(f32).reshape(1, feats), left_factor, right_factor, cotangent)
+    outs = hand_over(outs, chunks)
     return (*outs[:4], outs[4].reshape(feats))
 
 

time: 307 us -> 298 us (0.971)
  local copies, waits for them, and re-layouts: 7.88 us -> 0 us
    unnamed x13 -> x0, local copies, waits for them, and re-layouts: 7.88 us -> none
    pallas_call x1, Pallas kernels: 297 us -> 290 us  [fast(): pl.pallas_call(kernel, out_shape=(jax.ShapeDtypeStruct((rows, feats), bf1...]
    pallas_call x0 -> x1, Pallas kernels: none -> 6.26 us  [hand_over(): pl.pallas_call(kernel, out_shape=tuple((jax.ShapeDtypeStruct(a.shape, a.d...]
where the time goes in v2:
time: 298 us
  Pallas kernels  296 us (99%)
    pallas_call x1, Pallas kernels, fast(): pl.pallas_call(kernel, out_shape=(jax.ShapeDtypeStruct((rows, feats), bf1...  290 us
    pallas_call x1, Pallas kernels, hand_over(): pl.pallas_call(kernel, out_shape=tuple((jax.ShapeDtypeStruct(a.shape, a.d...  6.26 us

profile of v2, /device:TPU:0, one launch (start us, length us, event | category | flops | bytes accessed | tf_op | source)
XLA Modules:
  0.0 297.7 jit_solution(8499731533954031911)
XLA Ops:
  0.6 1.3 reshape.21
  1.9 289.5 %monarch.1 = (bf16[1536,1024]{1,0:T(8,128)(2,1)}, bf16[1536,1024]{1,0:T(8,128)(2,1)}, f32[8,128,128]{2,1,0:T(8,128)}, f32[8,128,128]{2,1,0:T(8,128)}, f32[1,1024]{1,0:T(1,128)}) custom-call(bf16[1536,1024]{1,0:T(8,128)(2,1)} %tok_hbm.1, f32[1,1024]{1,0:T(1,128)} %bitcast.2, bf16[8,128,128]{2,1,0:T(8,128)(2,1)} %left.1, bf16[8,128,128]{2,1,0:T(8,128)(2,1)} %right.1, ...), custom_call_target="tpu_custom_call" | custom-call | flops 32212254720 | bytes 12582912 | tf_op jit(solution)/shard_map/monarch/pallas_call | solution.py:463
  291.4 6.3 %hand_over.1 = (bf16[1536,1024]{1,0:T(8,128)(2,1)}, bf16[1536,1024]{1,0:T(8,128)(2,1)}, f32[8,128,128]{2,1,0:T(8,128)}, f32[8,128,128]{2,1,0:T(8,128)}, f32[1,1024]{1,0:T(1,128)}) custom-call(bf16[1536,1024]{1,0:T(8,128)(2,1)} %get-tuple-element.15.refs_0_, bf16[1536,1024]{1,0:T(8,128)(2,1)} %get-tuple-element.16.refs_1_, ...), custom_call_target="tpu_custom_call" | custom-call | tf_op jit(solution)/shard_map/hand_over/pallas_call | solution.py:87
